TPU v7x, 512 devices: a whole 4x8x8 slice. The times are simulated.
512 devices in a mesh: sx: 16 (over z_lo, y), sy: 32 (over x, z_hi, core).
Axes of the slice: x: 4, y: 8, z: 8 (z_hi: 4, z_lo: 2; z = z_hi * 2 + z_lo), core: 2. Of those that a mesh axis runs over, the one named last changes fastest.
Arguments:
- forward_weights: float32 [4096, 8, 432], P(('sy', 'sx')), may hold values from -6 to 6
- adjoint_weights: float32 [32768, 432], P(('sx', 'sy')), may hold values from -6 to 6
- medium: float32 [4], replicated, may hold values from 0.2 to 0.6
Outputs:
- forward_out: float32 [32768, 432], P(('sx', 'sy'))
- adjoint_out: float32 [8, 4096, 432], P(None, ('sy', 'sx'))
All inputs are finite; a program needn't handle non-finite values.
Results may differ from a plain program's by a relative error of at most 0.0003.
Values sent between devices are 32-bit elements; how exact they have to be, the bound alone decides.
No kernel may reach another device: no remote copies, remote signals or barrier semaphores. Data moves between devices by JAX's collectives and lax.ppermute only.
A program may use at most 64 MiB of HBM per device.

v0:
```python
import math
import jax
import jax.numpy as jnp
import numpy as np
from jax import lax
from jax.sharding import Mesh
from jax.sharding import PartitionSpec as P

ORDER = 6
LEVELS = 4
Q = 216
SY = ("sy_0", "sy_1", "sy_2")
SY_SX = ("sy_0", "sy_1", "sy_2", "sx")
SX_SY = ("sx", "sy_0", "sy_1", "sy_2")
two_pi = 2.0 * math.pi
shrink = 1.0 / math.sqrt(8.0)
band = 8.0


def in_blocks(x, dim, size):
    dims = x.shape
    pieces = x.reshape(*dims[:dim], size, dims[dim] // size, *dims[dim + 1 :])
    return jnp.moveaxis(pieces, dim, 0)


def in_order(pieces, dim):
    pieces = jnp.moveaxis(pieces, 0, dim)
    dims = pieces.shape
    return pieces.reshape(*dims[:dim], dims[dim] * dims[dim + 1], *dims[dim + 2 :])


def exchange_in_order(pieces, axes, sequence):
    inside = pieces.shape[1:]
    result = pieces.reshape(*(lax.axis_size(a) for a in axes), *inside)
    for k in sequence:
        result = lax.all_to_all(result, axes[k], k, k, tiled=True)
    return result.reshape(-1, *inside)


def two_step_exchange(x, groups, sequence, split_dim, concat_dim):
    size = lax.axis_size(groups[0]) * lax.axis_size(groups[1])
    pieces = in_blocks(x, split_dim, size)
    return in_order(exchange_in_order(pieces, groups, sequence), concat_dim)


def cheb_points(order_count):
    return np.array(
        [
            (1.0 - math.cos((2 * node_index + 1) * math.pi / (2 * order_count))) / 2.0
            for node_index in range(order_count)
        ]
    )


def child_table(order_count):
    nodes_here = cheb_points(order_count)
    halves = []
    for offset_bit in range(2):
        matrix = np.zeros((order_count, order_count))
        for row_index in range(order_count):
            where_at = (nodes_here[row_index] + offset_bit) / 2.0
            for col_index in range(order_count):
                value_now = 1.0
                for other_index in range(order_count):
                    if other_index != col_index:
                        value_now *= (where_at - nodes_here[other_index]) / (
                            nodes_here[col_index] - nodes_here[other_index]
                        )
                matrix[row_index, col_index] = value_now
        halves.append(matrix)
    blocks_out = []
    for child_index in range(8):
        along_x = halves[child_index // 4]
        along_y = halves[child_index // 2 % 2]
        along_z = halves[child_index % 2]
        blocks_out.append(np.kron(np.kron(along_x, along_y), along_z))
    return jnp.asarray(np.stack(blocks_out), dtype=jnp.float32)


def box_digits(box_index, groups):
    coord_x = jnp.zeros_like(box_index)
    coord_y = jnp.zeros_like(box_index)
    coord_z = jnp.zeros_like(box_index)
    for group_now in range(groups):
        digit_now = box_index // 8 ** (groups - 1 - group_now) % 8
        coord_x = coord_x * 2 + digit_now // 4
        coord_y = coord_y * 2 + digit_now // 2 % 2
        coord_z = coord_z * 2 + digit_now % 2
    return jnp.stack([coord_x, coord_y, coord_z], axis=-1).astype(jnp.float32)


def box_centres(box_index, groups):
    return (box_digits(box_index, groups) + 0.5) / float(2**groups)


def box_points(box_index, groups):
    box_side = band / float(2**groups)
    nodes_here = jnp.asarray(cheb_points(ORDER), dtype=jnp.float32)
    grid_x = jnp.repeat(nodes_here, ORDER * ORDER)
    grid_y = jnp.tile(jnp.repeat(nodes_here, ORDER), ORDER)
    grid_z = jnp.tile(nodes_here, ORDER * ORDER)
    offsets = jnp.stack([grid_x, grid_y, grid_z], axis=-1)
    corner = box_digits(box_index, groups)
    return box_side * (corner[..., None, :] + offsets)


def phase_angle(centres, points, medium):
    along = jnp.sum(centres * points, axis=-1)
    radius = jnp.sqrt(jnp.sum(points * points, axis=-1))
    travel = medium[0] + jnp.sum(medium[1:] * centres, axis=-1)
    return two_pi * (along + travel * radius)


def complex_turn(real_part, imag_part, angle_now, sign_now):
    cosine = jnp.cos(angle_now)
    sine_part = sign_now * jnp.sin(angle_now)
    return (real_part * cosine - imag_part * sine_part, real_part * sine_part + imag_part * cosine)


def forward_level(weights, src_off, tgt_off, level_now, medium, interp):
    src_count, tgt_count = (weights.shape[0], weights.shape[1])
    shot_count, point_count = (weights.shape[3], weights.shape[4])
    parent_count = src_count // 8
    new_targets = tgt_off * 8 + jnp.arange(tgt_count * 8, dtype=jnp.int32)
    centres = box_centres(new_targets, level_now + 2).reshape(tgt_count, 8, 3)
    children = src_off + jnp.arange(src_count, dtype=jnp.int32)
    child_points = box_points(children, LEVELS - level_now).reshape(parent_count, 8, point_count, 3)
    parents = src_off // 8 + jnp.arange(parent_count, dtype=jnp.int32)
    parent_points = box_points(parents, LEVELS - level_now - 1)
    theta_in = phase_angle(
        centres[None, None, :, :, None, :], child_points[:, :, None, None, :, :], medium
    )
    theta_out = phase_angle(
        centres[None, :, :, None, :], parent_points[:, None, None, :, :], medium
    )
    shaped = weights.reshape(parent_count, 8, tgt_count, 1, 2, shot_count, point_count)
    turned = complex_turn(
        shaped[:, :, :, :, 0], shaped[:, :, :, :, 1], theta_in[:, :, :, :, None, :], 1.0
    )
    stacked = jnp.stack(turned, axis=4)
    mixed = jnp.einsum("pctkxhq,cqs->ptkxhs", stacked, interp, precision=lax.Precision.HIGHEST)
    result_re, result_im = complex_turn(
        mixed[:, :, :, 0], mixed[:, :, :, 1], theta_out[:, :, :, None, :], -1.0
    )
    output = shrink * jnp.stack([result_re, result_im], axis=3)
    return output.reshape(parent_count, tgt_count * 8, 2, shot_count, point_count)


def adjoint_level(values, tgt_off, src_off, level_now, medium, interp):
    tgt_count, src_count = (values.shape[0], values.shape[1])
    shot_count, point_count = (values.shape[3], values.shape[4])
    parent_count = tgt_count // 8
    targets = tgt_off + jnp.arange(tgt_count, dtype=jnp.int32)
    centres = box_centres(targets, level_now + 2).reshape(parent_count, 8, 3)
    sources = src_off + jnp.arange(src_count, dtype=jnp.int32)
    source_points = box_points(sources, LEVELS - level_now - 1)
    children = src_off * 8 + jnp.arange(src_count * 8, dtype=jnp.int32)
    child_points = box_points(children, LEVELS - level_now).reshape(src_count, 8, point_count, 3)
    theta_out = phase_angle(
        centres[:, :, None, None, :], source_points[None, None, :, :, :], medium
    )
    theta_in = phase_angle(
        centres[:, :, None, None, None, :], child_points[None, None, :, :, :, :], medium
    )
    shaped = values.reshape(parent_count, 8, src_count, 2, shot_count, point_count)
    turned = complex_turn(shaped[:, :, :, 0], shaped[:, :, :, 1], theta_out[:, :, :, None, :], 1.0)
    stacked = jnp.stack(turned, axis=3)
    spread = jnp.einsum("pkbxhs,cqs->pkbcxhq", stacked, interp, precision=lax.Precision.HIGHEST)
    back_re, back_im = complex_turn(
        spread[:, :, :, :, 0], spread[:, :, :, :, 1], theta_in[:, :, :, :, None, :], -1.0
    )
    output = shrink * jnp.stack([jnp.sum(back_re, axis=1), jnp.sum(back_im, axis=1)], axis=3)
    return output.reshape(parent_count, src_count * 8, 2, shot_count, point_count)


def flatten_pairs(array_now):
    return array_now.reshape(array_now.shape[0], array_now.shape[1], -1)


def unfold_pairs(array_now):
    return array_now.reshape(array_now.shape[0], array_now.shape[1], 2, -1, Q)


def forward_moved(state_in, moved_array, axis_index):
    array_now, src_off, tgt_off, level_now = state_in
    return (
        moved_array,
        src_off - axis_index * array_now.shape[0],
        tgt_off + axis_index * moved_array.shape[1],
        level_now,
    )


def adjoint_moved(state_in, moved_array, axis_index):
    array_now, tgt_off, src_off, level_now = state_in
    return (
        moved_array,
        tgt_off - axis_index * array_now.shape[0],
        src_off + axis_index * moved_array.shape[1],
        level_now,
    )


def forward_steps(state_in, operations, medium, interp, index_x):
    for operation in operations:
        array_now, src_off, tgt_off, level_now = state_in
        if operation == "level":
            state_in = (
                forward_level(array_now, src_off, tgt_off, level_now, medium, interp),
                src_off // 8,
                tgt_off * 8,
                level_now + 1,
            )
        else:
            moved_array = unfold_pairs(
                lax.all_to_all(
                    flatten_pairs(array_now), "sx", split_axis=1, concat_axis=0, tiled=True
                )
            )
            state_in = forward_moved(state_in, moved_array, index_x)
    return state_in


def adjoint_steps(state_in, operations, medium, interp, index_x):
    for operation in operations:
        array_now, tgt_off, src_off, level_now = state_in
        if operation == "level":
            state_in = (
                adjoint_level(array_now, tgt_off, src_off, level_now - 1, medium, interp),
                tgt_off // 8,
                src_off * 8,
                level_now - 1,
            )
        else:
            moved_array = unfold_pairs(
                lax.all_to_all(
                    flatten_pairs(array_now), "sx", split_axis=1, concat_axis=0, tiled=True
                )
            )
            state_in = adjoint_moved(state_in, moved_array, index_x)
    return state_in


def shards(forward_weights, adjoint_weights, medium):
    interp = child_table(ORDER)
    size_x = lax.axis_size("sx")
    size_y = lax.axis_size(SY)
    index_x = lax.axis_index("sx")
    index_y = lax.axis_index(SY)
    local_sources = forward_weights.shape[0]
    plan_ops = []
    remaining = [("sx", size_x), ("sy", size_y)]
    local_width = local_sources
    for level_now in range(LEVELS):
        while local_width < 8:
            axis_name, axis_size = remaining.pop(0)
            plan_ops.append(axis_name)
            local_width = local_width * axis_size
        plan_ops.append("level")
        local_width = local_width // 8
    cut_at = plan_ops.index("sy")
    early_ops = plan_ops[:cut_at]
    late_ops = plan_ops[cut_at + 1 :]
    forward_state = (
        unfold_pairs(forward_weights),
        (index_y * size_x + index_x) * local_sources,
        jnp.int32(0),
        0,
    )
    back_state = (
        unfold_pairs(adjoint_weights[:, None]),
        (index_x * size_y + index_y) * adjoint_weights.shape[0],
        jnp.int32(0),
        LEVELS,
    )
    forward_state = forward_steps(forward_state, early_ops, medium, interp, index_x)
    back_state = adjoint_steps(back_state, list(reversed(late_ops)), medium, interp, index_x)
    moved_forward, moved_back = (
        two_step_exchange(
            flatten_pairs(forward_state[0]), (("sy_0", "sy_1"), "sy_2"), (1, 0), 1, 0
        ),
        two_step_exchange(flatten_pairs(back_state[0]), (("sy_0", "sy_1"), "sy_2"), (1, 0), 1, 0),
    )
    forward_state = forward_moved(forward_state, unfold_pairs(moved_forward), index_y)
    back_state = adjoint_moved(back_state, unfold_pairs(moved_back), index_y)
    forward_state = forward_steps(forward_state, late_ops, medium, interp, index_x)
    back_state = adjoint_steps(back_state, list(reversed(early_ops)), medium, interp, index_x)
    forward_out = forward_state[0].reshape(forward_state[0].shape[1], -1)
    return (forward_out, flatten_pairs(back_state[0]))


def solution(mesh):
    split = Mesh(mesh.devices.reshape(mesh.shape["sx"], 4, 4, 2), ("sx", "sy_0", "sy_1", "sy_2"))
    return jax.shard_map(
        shards,
        mesh=split,
        in_specs=(P(SY_SX, None, None), P(SX_SY, None), P()),
        out_specs=(P(SX_SY, None), P(None, SY_SX, None)),
        check_vma=False,
    )
```

profile of v0, /device:TPU:2, one launch (start us, length us, event | category | flops | bytes accessed | tf_op | source)
XLA Modules:
  0.0 162.8 jit_solution(14685372909776085606)
XLA Ops:
  2.7 0.7 tile.98
  3.6 0.7 broadcast_in_dim.65
  4.6 0.7 broadcast_in_dim.64
  7.6 0.7 broadcast_multiply_fusion.1
  8.6 1.1 reshape_reshape_broadcast_in_dim.3
  10.9 0.7 multiply_reduce_fusion.8
  12.0 2.1 %convolution_bitcast_fusion.3 = f32[8,8,1,8,2,1,216]{6,1,4,0,3,5,2:T(8,128)S(1)} fusion(f32[8,216,216,1,1]{2,1,4,3,0:T(8,128)S(1)} %copy-done.1, f32[8,8,1,1,1,216]{5,1,3,0,4,2:T(8,128)S(1)} %get-tuple-element.31, f32[8,8,1,1,1,216]{5,1,3,0,4,2:T(8,128)S(1)} %get-tuple-element.30), kind=kOutput, calls=%fused_computation.11 | convolution fusion | flops 573336576 | bytes 2488320 | tf_op jit(solution)/shard_map/pkbxhs,cqs->pkbcxhq/dot_general | solution.py:168
  14.1 2.7 %subtract_reduce_fusion.3 = (f32[8,8,216]{2,0,1:T(8,128)S(1)}, f32[8,8,216]{2,0,1:T(8,128)S(1)}) fusion(f32[8,8,1,8,2,1,216]{6,1,4,0,3,5,2:T(8,128)S(1)} %convolution_bitcast_fusion.3, f32[8,8,8,216]{3,2,1,0:T(8,128)S(1)} %multiply_reduce_fusion.3, f32[8,216]{1,0:T(8,128)S(1)} %sqrt.137, f32[8,8]{1,0:T(8,128)S(1)} %broadcast_add_fusion.6), kind=kLoop, calls=%fused_computation.62 | loop fusion | flops 1299456 | bytes 1444864 | tf_op jit(solution)/shard_map/reduce_sum | solution.py:172
  18.2 2.1 %convolution_bitcast_fusion.2 = f32[1,8,8,8,2,1,216]{6,2,4,1,3,5,0:T(8,128)S(1)} fusion(f32[8,216,216,1,1]{2,1,4,3,0:T(8,128)S(1)} %copy-done.1, f32[1,8,8,1,1,216]{5,2,3,1,4,0:T(8,128)S(1)} %get-tuple-element.27, f32[1,8,8,1,1,216]{5,2,3,1,4,0:T(8,128)S(1)} %get-tuple-element.26), kind=kOutput, calls=%fused_computation.10 | convolution fusion | flops 573336576 | bytes 2488320 | tf_op jit(solution)/shard_map/pkbxhs,cqs->pkbcxhq/dot_general | solution.py:168
  20.3 2.5 %subtract_reduce_fusion.2 = (f32[8,8,216]{2,0,1:T(8,128)S(1)}, f32[8,8,216]{2,0,1:T(8,128)S(1)}) fusion(f32[1,8,8,8,2,1,216]{6,2,4,1,3,5,0:T(8,128)S(1)} %convolution_bitcast_fusion.2, f32[8,8,8,216]{3,2,1,0:T(8,128)S(1)} %multiply_reduce_fusion.2, f32[8,8,216]{2,0,1:T(8,128)S(1)} %copy.435, f32[8]{0:T(128)S(1)} %get-tuple-element.119), kind=kLoop, calls=%fused_computation.59 | loop fusion | flops 1299456 | bytes 1493024 | tf_op jit(solution)/shard_map/reduce_sum | solution.py:172
  23.2 3.8 %all_to_all.44 = f32[16,2,1,2,432]{4,3,0,2,1:T(2,128)S(1)} all-to-all(f32[16,2,1,2,432]{4,3,0,2,1:T(2,128)S(1)} %copy.439), channel_id=1, replica_groups=mesh['sx'=16,'sy_0'=4,'sy_1'=4,'sy_2'=2] {'sy_2'}, dimensions={1} | all-to-all | bytes 221184 | tf_op jit(solution)/shard_map/all_to_all | solution.py:36
  27.1 0.7 copy.440
  27.7 13.3 %all-to-all-start.4 = ((f32[16,2,1,2,432]{4,3,1,2,0:T(2,128)}), f32[16,2,1,2,432]{4,3,1,2,0:T(2,128)S(1)}, u32[]{:S(2)}, u32[]{:S(2)}) async-start(f32[16,2,1,2,432]{4,3,1,2,0:T(2,128)} %copy.440), calls=%async_computation.4 | async-start | bytes 262144 | tf_op jit(solution)/shard_map/all_to_all | solution.py:36
  49.4 0.7 copy.446
  50.4 0.7 multiply_reduce_fusion.23
  51.4 0.7 broadcast_add_fusion
  52.6 0.7 multiply_reduce_fusion.15
  54.5 0.7 multiply_reduce_fusion.24
  61.0 0.7 multiply_reduce_fusion.13
  61.9 2.0 %multiply_subtract_fusion.3 = (f32[1,8,8,8,1,1,216]{6,3,1,4,2,5,0:T(8,128)S(1)}, f32[1,8,8,8,1,1,216]{6,3,1,4,2,5,0:T(8,128)S(1)}) fusion(f32[8,8,8,216]{3,2,1,0:T(8,128)S(1)} %multiply_reduce_fusion.7, f32[8,8,216]{2,0,1:T(8,128)S(1)} %get-tuple-element.111, f32[8,216]{1,0:T(8,128)S(1)} %sqrt.128, f32[8,8]{1,0:T(8,128)S(1)} %broadcast_add_fusion.11, ...), kind=kLoop, calls=%fused_computation.71 | loop fusion | flops 995328 | bytes 1444864 | tf_op jit(solution)/shard_map/sub | solution.py:117
  64.0 1.4 convolution_bitcast_fusion.7
  65.8 1.0 mul.4774
  68.3 1.0 multiply_reduce_fusion.6
  69.3 0.7 multiply_reduce_fusion.16
  72.0 1.5 sqrt.132
  73.5 0.8 fusion.267
  74.8 0.7 sqrt.133
  75.6 1.3 sqrt.134
  76.9 0.8 fusion.69
  78.3 0.8 fusion.72
  81.3 0.7 multiply_reduce_fusion.9
  82.0 1.0 multiply_reduce_fusion.1
  83.1 0.8 fusion.270
  84.3 8.2 %all-to-all-start = ((f32[1,64,432]{2,0,1:T(1,128)}), f32[1,64,432]{2,0,1:T(1,128)}, u32[]{:S(2)}, u32[]{:S(2)}) async-start(f32[1,64,432]{2,0,1:T(1,128)} %mul.4774), calls=%async_computation | async-start | bytes 262144 | tf_op jit(solution)/shard_map/all_to_all | solution.py:216
  92.5 0.9 reshape_reshape_reshape_reshape.7
  93.4 1.7 %fusion.428 = (f32[4,8,2,1,1,216]{5,3,2,1,0,4:T(1,128)}, f32[4,8,2,1,1,216]{5,3,2,1,0,4:T(1,128)}) fusion(f32[4,8,2,2,1,216]{5,3,2,1,0,4:T(2,128)} %reshape_reshape_reshape_reshape.7), kind=kLoop, calls=%fused_computation.1350 | loop fusion | bytes 221184 | tf_op jit(solution)/shard_map/slice | solution.py:166
  95.1 6.0 %all-to-all-done = f32[1,64,432]{2,0,1:T(1,128)} async-done(((f32[1,64,432]{2,0,1:T(1,128)}), f32[1,64,432]{2,0,1:T(1,128)}, u32[]{:S(2)}, u32[]{:S(2)}) %all-to-all-start) | async-done | bytes 110624 | tf_op jit(solution)/shard_map/all_to_all | solution.py:216
  101.1 1.9 %reduce.52 = f32[64,432]{1,0:T(8,128)} reduce(f32[1,64,432]{2,0,1:T(1,128)} %all-to-all-done, f32[]{:T(128)} %constant.2451), dimensions={0}, to_apply=%all_to_all.30.reduce_sub_computation | reduce | bytes 221188 | tf_op jit(solution)/shard_map/all_to_all | solution.py:216
  103.0 1.1 reshape_reshape.7
  104.2 3.7 %multiply_subtract_fusion.2 = (f32[2,8,4,8,1,1,216]{6,3,1,4,2,0,5:T(8,128)S(1)}, f32[2,8,4,8,1,1,216]{6,3,1,4,2,0,5:T(8,128)S(1)}) fusion(f32[2,8,4,8,216]{4,3,2,1,0:T(8,128)} %multiply_reduce_fusion.6, f32[2,8,4,216]{3,1,2,0:T(8,128)S(1)} %bitcast.578, f32[2,8,216]{2,1,0:T(8,128)} %sqrt.130, f32[4,8]{1,0:T(4,128)} %broadcast_add_fusion.15, ...), kind=kLoop, calls=%fused_computation.69 | loop fusion | flops 995328 | bytes 1451648 | tf_op jit(solution)/shard_map/sub | solution.py:117
  108.0 1.4 convolution_bitcast_fusion.6
  109.9 0.8 mul.4489
  110.7 1.0 reshape.11716
  111.8 3.8 %all_to_all.45 = f32[16,2,2,1,432]{4,2,0,3,1:T(2,128)S(1)} all-to-all(f32[16,2,2,1,432]{4,2,0,3,1:T(2,128)S(1)} %copy.404), channel_id=1, replica_groups=mesh['sx'=16,'sy_0'=4,'sy_1'=4,'sy_2'=2] {'sy_2'}, dimensions={1} | all-to-all | bytes 221184 | tf_op jit(solution)/shard_map/all_to_all | solution.py:36
  115.6 0.7 copy.405
  116.3 9.8 %all-to-all-start.2 = ((f32[16,2,2,1,432]{4,2,1,3,0:T(2,128)}), f32[16,2,2,1,432]{4,2,1,3,0:T(2,128)S(1)}, u32[]{:S(2)}, u32[]{:S(2)}) async-start(f32[16,2,2,1,432]{4,2,1,3,0:T(2,128)} %copy.405), calls=%async_computation.2 | async-start | bytes 262144 | tf_op jit(solution)/shard_map/all_to_all | solution.py:36
  126.1 1.3 multiply_subtract_fusion.5
  127.4 3.5 %convolution_bitcast_fusion.1 = f32[4,8,2,8,2,1,216]{6,1,4,2,0,3,5:T(8,128)S(1)} fusion(f32[8,216,216,1,1,1]{2,1,5,4,3,0:T(8,128)} %constant.2449, f32[4,8,2,1,1,216]{5,1,3,2,0,4:T(8,128)S(1)} %get-tuple-element.37, f32[4,8,2,1,1,216]{5,1,3,2,0,4:T(8,128)S(1)} %get-tuple-element.36), kind=kOutput, calls=%fused_computation.9 | convolution fusion | flops 573336576 | bytes 2488320 | tf_op jit(solution)/shard_map/pkbxhs,cqs->pkbcxhq/dot_general | solution.py:168
  131.0 2.8 %subtract_reduce_fusion.1 = (f32[4,2,8,216]{3,1,0,2:T(2,128)S(1)}, f32[4,2,8,216]{3,1,0,2:T(2,128)S(1)}) fusion(f32[4,8,2,8,2,1,216]{6,1,4,2,0,3,5:T(8,128)S(1)} %convolution_bitcast_fusion.1, f32[4,8,2,8,216]{4,3,2,1,0:T(8,128)S(1)} %copy-done.2, f32[2,8,216]{2,0,1:T(2,128)S(1)} %copy-done.10, f32[4,8]{1,0:T(4,128)S(1)} %copy-done.33), kind=kLoop, calls=%fused_computation.56 | loop fusion | flops 1299456 | bytes 1451648 | tf_op jit(solution)/shard_map/reduce_sum | solution.py:172
  133.9 0.7 copy.475
  134.6 1.7 %reshape.11733 = f32[4,16,432]{2,0,1:T(4,128)} reshape(f32[4,2,8,2,1,216]{5,3,0,2,1,4:T(2,128)} %copy.475) | data formatting | bytes 221184 | tf_op jit(solution)/shard_map/mul | solution.py:172
  136.3 4.4 %all-to-all-start.5 = ((f32[4,16,432]{2,0,1:T(4,128)}), f32[4,16,432]{2,0,1:T(4,128)}, u32[]{:S(2)}, u32[]{:S(2)}) async-start(f32[4,16,432]{2,0,1:T(4,128)} %reshape.11733), calls=%async_computation.5 | async-start | bytes 262144 | tf_op jit(solution)/shard_map/all_to_all | solution.py:236
  140.8 0.9 reshape_reshape_reshape_reshape.6
  141.6 1.1 fusion.430
  142.8 2.9 %multiply_subtract_fusion.1 = (f32[8,8,1,8,1,1,216]{6,3,1,4,0,5,2:T(8,128)S(1)}, f32[8,8,1,8,1,1,216]{6,3,1,4,0,5,2:T(8,128)S(1)}) fusion(f32[8,8,8,216]{3,2,1,0:T(8,128)S(1)} %multiply_reduce_fusion.5, f32[8,8,216]{2,1,0:T(8,128)S(1)} %bitcast.579, f32[8,8,216]{2,1,0:T(8,128)} %sqrt.132, f32[8]{0:T(128)S(1)} %copy-done.48, f32[8,8,216]{2,1,0:T(8,128)S(1)} %bitcast.581), kind=kLoop, calls=%fused_computation.67 | loop fusion | flops 995328 | bytes 1493024 | tf_op jit(solution)/shard_map/sub | solution.py:117
  145.7 1.4 convolution_bitcast_fusion.5
  147.8 1.4 all-to-all-done.5
  149.2 1.1 reshape_reshape.8
  150.7 3.5 %convolution_bitcast_fusion = f32[8,8,1,8,2,1,216]{6,1,0,3,5,4,2:T(8,128)S(1)} fusion(f32[8,216,216,1,1]{2,1,3,0,4:T(8,128)} %constant.2448, f32[8,8,1,1,1,216]{5,1,3,0,4,2:T(8,128)S(1)} %get-tuple-element.29, f32[8,8,1,1,1,216]{5,1,3,0,4,2:T(8,128)S(1)} %get-tuple-element.28), kind=kOutput, calls=%fused_computation.8 | convolution fusion | flops 573336576 | bytes 2488320 | tf_op jit(solution)/shard_map/pkbxhs,cqs->pkbcxhq/dot_general | solution.py:168
  154.3 2.7 %subtract_reduce_fusion = (f32[8,8,216]{2,0,1:T(8,128)S(1)}, f32[8,8,216]{2,0,1:T(8,128)S(1)}) fusion(f32[8,8,1,8,2,1,216]{6,1,0,3,5,4,2:T(8,128)S(1)} %convolution_bitcast_fusion, f32[8,8,8,216]{3,2,1,0:T(8,128)S(1)} %multiply_reduce_fusion, f32[8,216]{1,0:T(8,128)S(1)} %copy-done.12, f32[8,8]{1,0:T(8,128)S(1)} %copy-done.16), kind=kLoop, calls=%fused_computation.53 | loop fusion | flops 1299456 | bytes 1444864 | tf_op jit(solution)/shard_map/reduce_sum | solution.py:172
  157.2 0.8 mul.4773
  158.1 2.0 %multiply_subtract_fusion = (f32[1,8,8,8,1,1,216]{6,3,1,4,2,5,0:T(8,128)S(1)}, f32[1,8,8,8,1,1,216]{6,3,1,4,2,5,0:T(8,128)S(1)}) fusion(f32[8,8,8,216]{3,2,1,0:T(8,128)S(1)} %multiply_reduce_fusion.4, f32[8,8,216]{2,0,1:T(8,128)S(1)} %copy.418, f32[8,216]{1,0:T(8,128)S(1)} %copy-done.13, f32[8,8]{1,0:T(8,128)S(1)} %copy-done.15, f32[8,8,216]{2,0,1:T(8,128)S(1)} %copy.414), kind=kLoop, calls=%fused_computation.65 | loop fusion | flops 995328 | bytes 1444864 | tf_op jit(solution)/shard_map/sub | solution.py:117
  160.2 1.4 convolution_bitcast_fusion.4
  162.0 0.8 mul.4599
  (317 shorter events, 34.1 us)
Async XLA Ops:
  0.6 11.4 %copy-start.1 = (f32[8,216,216,1,1]{2,1,4,3,0:T(8,128)S(1)}, f32[8,216,216,1,1]{2,1,4,3,0:T(8,128)}, u32[]{:S(2)}) copy-start(f32[8,216,216,1,1]{2,1,4,3,0:T(8,128)} %constant.2450) | copy-start | bytes 4478980
  0.6 9.8 %copy-start.9 = (f32[4]{0:T(128)S(1)}, f32[4]{0:T(128)}, u32[]{:S(2)}) copy-start(f32[4]{0:T(128)} %param.22) | copy-start | bytes 52
  8.3 5.8 %copy-start.30 = (f32[3]{0:T(128)}, f32[3]{0:T(128)S(1)}, u32[]{:S(2)}) copy-start(f32[3]{0:T(128)S(1)} %get-tuple-element.67) | copy-start | bytes 40
  8.3 53.4 %copy-start.28 = (f32[3]{0:T(128)}, f32[3]{0:T(128)S(1)}, u32[]{:S(2)}) copy-start(f32[3]{0:T(128)S(1)} %get-tuple-element.70) | copy-start | bytes 40
  8.3 62.3 %copy-start.26 = (f32[3]{0:T(128)}, f32[3]{0:T(128)S(1)}, u32[]{:S(2)}) copy-start(f32[3]{0:T(128)S(1)} %get-tuple-element.68) | copy-start | bytes 40
  8.3 65.2 %copy-start.25 = (f32[3]{0:T(128)}, f32[3]{0:T(128)S(1)}, u32[]{:S(2)}) copy-start(f32[3]{0:T(128)S(1)} %get-tuple-element.69) | copy-start | bytes 40
  8.6 5.5 %copy-start.31 = (f32[216]{0:T(256)}, f32[216]{0:T(256)S(1)}, u32[]{:S(2)}) copy-start(f32[216]{0:T(256)S(1)} %sqrt.135) | copy-start | bytes 2596
  22.8 37.7 %copy-start.8 = (f32[8,8,432]{2,1,0:T(8,128)S(1)}, f32[8,8,432]{2,1,0:T(8,128)}, u32[]{:S(2)}) copy-start(f32[8,8,432]{2,1,0:T(8,128)} %param.20) | copy-start | bytes 331780
  27.7 56.6 %all-to-all-start.4 = ((f32[16,2,1,2,432]{4,3,1,2,0:T(2,128)}), f32[16,2,1,2,432]{4,3,1,2,0:T(2,128)S(1)}, u32[]{:S(2)}, u32[]{:S(2)}) async-start(f32[16,2,1,2,432]{4,3,1,2,0:T(2,128)} %copy.440), calls=%async_computation.4 | async-start | bytes 262144 | tf_op jit(solution)/shard_map/all_to_all | solution.py:36
  59.8 4.2 %copy-start = (f32[8,216,216,1,1]{2,1,0,4,3:T(8,128)S(1)}, f32[8,216,216,1,1]{2,1,0,4,3:T(8,128)}, u32[]{:S(2)}) copy-start(f32[8,216,216,1,1]{2,1,0,4,3:T(8,128)} %constant.2446) | copy-start | bytes 4478980
  66.7 12.9 %copy-start.20 = (s32[8,8,1,1,1]{1,0,4,3,2:T(8,128)S(1)}, s32[8,8,1,1,1]{1,0,4,3,2:T(8,128)}, u32[]{:S(2)}) copy-start(s32[8,8,1,1,1]{1,0,4,3,2:T(8,128)} %fusion.298) | copy-start | bytes 772
  66.7 12.9 %copy-start.21 = (s32[8,8,1,1,1]{1,0,4,3,2:T(8,128)S(1)}, s32[8,8,1,1,1]{1,0,4,3,2:T(8,128)}, u32[]{:S(2)}) copy-start(s32[8,8,1,1,1]{1,0,4,3,2:T(8,128)} %fusion.300) | copy-start | bytes 772
  66.8 12.9 %copy-start.22 = (s32[8,8,1,1,1]{1,0,4,3,2:T(8,128)S(1)}, s32[8,8,1,1,1]{1,0,4,3,2:T(8,128)}, u32[]{:S(2)}) copy-start(s32[8,8,1,1,1]{1,0,4,3,2:T(8,128)} %fusion.302) | copy-start | bytes 772
  66.8 12.9 %copy-start.29 = (f32[3]{0:T(128)S(1)}, f32[3]{0:T(128)}, u32[]{:S(2)}) copy-start(f32[3]{0:T(128)} %copy-done.28) | copy-start | bytes 40
  66.8 13.0 %copy-start.17 = (s32[8,8,1,1,1,1]{1,0,5,4,3,2:T(8,128)S(1)}, s32[8,8,1,1,1,1]{1,0,5,4,3,2:T(8,128)}, u32[]{:S(2)}) copy-start(s32[8,8,1,1,1,1]{1,0,5,4,3,2:T(8,128)} %fusion.297) | copy-start | bytes 772
  66.8 13.0 %copy-start.18 = (s32[8,8,1,1,1,1]{1,0,5,4,3,2:T(8,128)S(1)}, s32[8,8,1,1,1,1]{1,0,5,4,3,2:T(8,128)}, u32[]{:S(2)}) copy-start(s32[8,8,1,1,1,1]{1,0,5,4,3,2:T(8,128)} %fusion.299) | copy-start | bytes 772
  66.8 13.0 %copy-start.19 = (s32[8,8,1,1,1,1]{1,0,5,4,3,2:T(8,128)S(1)}, s32[8,8,1,1,1,1]{1,0,5,4,3,2:T(8,128)}, u32[]{:S(2)}) copy-start(s32[8,8,1,1,1,1]{1,0,5,4,3,2:T(8,128)} %fusion.301) | copy-start | bytes 772
  66.8 13.7 %copy-start.37 = (s32[4,8,1,1,1,1]{1,0,5,4,3,2:T(4,128)S(1)}, s32[4,8,1,1,1,1]{1,0,5,4,3,2:T(4,128)}, u32[]{:S(2)}) copy-start(s32[4,8,1,1,1,1]{1,0,5,4,3,2:T(4,128)} %fusion.329) | copy-start | bytes 388
  66.8 13.7 %copy-start.38 = (s32[4,8,1,1,1,1]{1,0,5,4,3,2:T(4,128)S(1)}, s32[4,8,1,1,1,1]{1,0,5,4,3,2:T(4,128)}, u32[]{:S(2)}) copy-start(s32[4,8,1,1,1,1]{1,0,5,4,3,2:T(4,128)} %fusion.331) | copy-start | bytes 388
  66.8 13.7 %copy-start.39 = (s32[4,8,1,1,1,1]{1,0,5,4,3,2:T(4,128)S(1)}, s32[4,8,1,1,1,1]{1,0,5,4,3,2:T(4,128)}, u32[]{:S(2)}) copy-start(s32[4,8,1,1,1,1]{1,0,5,4,3,2:T(4,128)} %fusion.333) | copy-start | bytes 388
  66.8 13.8 %copy-start.34 = (s32[4,8,1,1,1]{1,0,4,3,2:T(4,128)S(1)}, s32[4,8,1,1,1]{1,0,4,3,2:T(4,128)}, u32[]{:S(2)}) copy-start(s32[4,8,1,1,1]{1,0,4,3,2:T(4,128)} %fusion.330) | copy-start | bytes 388
  66.8 13.8 %copy-start.35 = (s32[4,8,1,1,1]{1,0,4,3,2:T(4,128)S(1)}, s32[4,8,1,1,1]{1,0,4,3,2:T(4,128)}, u32[]{:S(2)}) copy-start(s32[4,8,1,1,1]{1,0,4,3,2:T(4,128)} %fusion.332) | copy-start | bytes 388
  66.8 13.8 %copy-start.36 = (s32[4,8,1,1,1]{1,0,4,3,2:T(4,128)S(1)}, s32[4,8,1,1,1]{1,0,4,3,2:T(4,128)}, u32[]{:S(2)}) copy-start(s32[4,8,1,1,1]{1,0,4,3,2:T(4,128)} %fusion.334) | copy-start | bytes 388
  66.8 14.5 %copy-start.14 = (f32[4,8,3]{1,2,0:T(4,128)S(1)}, f32[4,8,3]{1,2,0:T(4,128)}, u32[]{:S(2)}) copy-start(f32[4,8,3]{1,2,0:T(4,128)} %copy.442) | copy-start | bytes 1156
  66.9 15.2 %copy-start.7 = (f32[2,8,216,3]{2,1,3,0:T(8,128)S(1)}, f32[2,8,216,3]{2,1,3,0:T(8,128)}, u32[]{:S(2)}) copy-start(f32[2,8,216,3]{2,1,3,0:T(8,128)} %get-tuple-element.54) | copy-start | bytes 124420
  66.9 15.2 %copy-start.11 = (f32[4,8,3]{2,1,0:T(8,128)S(1)}, f32[4,8,3]{2,1,0:T(8,128)}, u32[]{:S(2)}) copy-start(f32[4,8,3]{2,1,0:T(8,128)} %copy.446) | copy-start | bytes 1156
  68.3 14.8 %copy-start.45 = (s32[1,1,8,1,1]{2,4,3,1,0:T(1,128)S(1)}, s32[1,1,8,1,1]{2,4,3,1,0:T(1,128)}, u32[]{:S(2)}) copy-start(s32[1,1,8,1,1]{2,4,3,1,0:T(1,128)} %get-tuple-element.107) | copy-start | bytes 100
  68.3 14.8 %copy-start.46 = (s32[1,1,8,1,1]{2,4,3,1,0:T(1,128)S(1)}, s32[1,1,8,1,1]{2,4,3,1,0:T(1,128)}, u32[]{:S(2)}) copy-start(s32[1,1,8,1,1]{2,4,3,1,0:T(1,128)} %get-tuple-element.108) | copy-start | bytes 100
  68.3 14.8 %copy-start.47 = (s32[1,1,8,1,1]{2,4,3,1,0:T(1,128)S(1)}, s32[1,1,8,1,1]{2,4,3,1,0:T(1,128)}, u32[]{:S(2)}) copy-start(s32[1,1,8,1,1]{2,4,3,1,0:T(1,128)} %fusion.425) | copy-start | bytes 100
  70.7 9.8 %copy-start.27 = (f32[3]{0:T(128)S(1)}, f32[3]{0:T(128)}, u32[]{:S(2)}) copy-start(f32[3]{0:T(128)} %copy-done.26) | copy-start | bytes 40
  84.3 16.8 %all-to-all-start = ((f32[1,64,432]{2,0,1:T(1,128)}), f32[1,64,432]{2,0,1:T(1,128)}, u32[]{:S(2)}, u32[]{:S(2)}) async-start(f32[1,64,432]{2,0,1:T(1,128)} %mul.4774), calls=%async_computation | async-start | bytes 262144 | tf_op jit(solution)/shard_map/all_to_all | solution.py:216
  104.1 3.9 %copy-start.3 = (f32[8,216,216,1,1,1]{2,1,0,5,4,3:T(8,128)S(1)}, f32[8,216,216,1,1,1]{2,1,0,5,4,3:T(8,128)}, u32[]{:S(2)}) copy-start(f32[8,216,216,1,1,1]{2,1,0,5,4,3:T(8,128)} %constant.2447) | copy-start | bytes 4478980
  108.0 1.4 copy-start.4
  108.0 1.4 copy-start.41
  108.0 1.4 copy-start.42
  109.4 16.6 %copy-start.40 = (f32[4,8]{1,0:T(4,128)S(1)}, f32[4,8]{1,0:T(4,128)}, u32[]{:S(2)}) copy-start(f32[4,8]{1,0:T(4,128)} %get-tuple-element.118) | copy-start | bytes 388
  116.3 14.6 %copy-start.33 = (f32[4,8]{1,0:T(4,128)S(1)}, f32[4,8]{1,0:T(4,128)}, u32[]{:S(2)}) copy-start(f32[4,8]{1,0:T(4,128)} %get-tuple-element.117) | copy-start | bytes 388
  116.3 20.0 %all-to-all-start.2 = ((f32[16,2,2,1,432]{4,2,1,3,0:T(2,128)}), f32[16,2,2,1,432]{4,2,1,3,0:T(2,128)S(1)}, u32[]{:S(2)}, u32[]{:S(2)}) async-start(f32[16,2,2,1,432]{4,2,1,3,0:T(2,128)} %copy.405), calls=%async_computation.2 | async-start | bytes 262144 | tf_op jit(solution)/shard_map/all_to_all | solution.py:36
  126.1 4.9 %copy-start.2 = (f32[4,8,2,8,216]{4,3,2,1,0:T(8,128)S(1)}, f32[4,8,2,8,216]{4,3,2,1,0:T(8,128)}, u32[]{:S(2)}) copy-start(f32[4,8,2,8,216]{4,3,2,1,0:T(8,128)} %multiply_reduce_fusion.1) | copy-start | bytes 1327108
  126.1 4.9 %copy-start.10 = (f32[2,8,216]{2,0,1:T(2,128)S(1)}, f32[2,8,216]{2,0,1:T(2,128)}, u32[]{:S(2)}) copy-start(f32[2,8,216]{2,0,1:T(2,128)} %copy.450) | copy-start | bytes 41476
  130.9 11.8 %copy-start.48 = (f32[8]{0:T(128)S(1)}, f32[8]{0:T(128)}, u32[]{:S(2)}) copy-start(f32[8]{0:T(128)} %broadcast_add_fusion.19) | copy-start | bytes 100
  136.3 12.8 %all-to-all-start.5 = ((f32[4,16,432]{2,0,1:T(4,128)}), f32[4,16,432]{2,0,1:T(4,128)}, u32[]{:S(2)}, u32[]{:S(2)}) async-start(f32[4,16,432]{2,0,1:T(4,128)} %reshape.11733), calls=%async_computation.5 | async-start | bytes 262144 | tf_op jit(solution)/shard_map/all_to_all | solution.py:236
  145.7 1.4 copy-start.44
  145.7 4.7 %copy-start.5 = (f32[8,8,216]{2,1,0:T(8,128)S(1)}, f32[8,8,216]{2,1,0:T(8,128)}, u32[]{:S(2)}) copy-start(f32[8,8,216]{2,1,0:T(8,128)} %get-tuple-element.77) | copy-start | bytes 165892
  145.7 4.7 %copy-start.24 = (f32[8,8]{1,0:T(8,128)S(1)}, f32[8,8]{1,0:T(8,128)}, u32[]{:S(2)}) copy-start(f32[8,8]{1,0:T(8,128)} %get-tuple-element.116) | copy-start | bytes 772
  145.7 4.7 %copy-start.43 = (f32[216]{0:T(256)S(1)}, f32[216]{0:T(256)}, u32[]{:S(2)}) copy-start(f32[216]{0:T(256)} %sqrt.142) | copy-start | bytes 2596
  150.2 4.1 %copy-start.12 = (f32[8,216]{1,0:T(8,128)S(1)}, f32[8,216]{1,0:T(8,128)}, u32[]{:S(2)}) copy-start(f32[8,216]{1,0:T(8,128)} %sqrt.143) | copy-start | bytes 20740
  150.3 4.1 %copy-start.16 = (f32[8,8]{1,0:T(8,128)S(1)}, f32[8,8]{1,0:T(8,128)}, u32[]{:S(2)}) copy-start(f32[8,8]{1,0:T(8,128)} %get-tuple-element.115) | copy-start | bytes 772
  154.3 3.8 %copy-start.13 = (f32[8,216]{1,0:T(8,128)S(1)}, f32[8,216]{1,0:T(8,128)}, u32[]{:S(2)}) copy-start(f32[8,216]{1,0:T(8,128)} %sqrt.134) | copy-start | bytes 20740
  154.3 3.8 %copy-start.15 = (f32[8,8]{1,0:T(8,128)S(1)}, f32[8,8]{1,0:T(8,128)}, u32[]{:S(2)}) copy-start(f32[8,8]{1,0:T(8,128)} %broadcast_add_fusion.9) | copy-start | bytes 772
  160.1 1.4 copy-start.6
  160.2 1.4 copy-start.23
  160.2 1.4 copy-start.32
where the time goes:
time: 164 us; the launch traced here: 163 us
  other arithmetic  62.9 us (38%)
  starting transfers between devices  35.7 us (22%)
  local copies, waits for them, and re-layouts  29.5 us (18%)
  matrix products  16.7 us (10%)
  blocking collectives  7.68 us (5%)
  waiting for transfers between devices  7.42 us (5%)
  between operations  2.96 us (2%)
    all_to_all x2, starting transfers between devices, exchange_in_order(): result = lax.all_to_all(result, axes[k], k, k, tiled=True)  23.1 us
    another operation x38, other arithmetic, box_digits(): return jnp.stack([coord_x, coord_y, coord_z], axis=-1).astype(jnp.float32)  14.1 us
    sub x11, other arithmetic, complex_turn(): real_part * cosine - imag_part * sine_part  13.9 us
    dot_general x4, matrix products, adjoint_level(): jnp.einsum('pkbxhs,cqs->pkbcxhq', stacked, interp, precision=lax.Precisio...  11.2 us
    reduce_sum x4, other arithmetic, adjoint_level(): jnp.sum(back_re, axis=1)  10.8 us
    all_to_all x1, starting transfers between devices, forward_steps(): lax.all_to_all(flatten_pairs(array_now), 'sx', split_axis=1, concat_axis=...  8.18 us
    all_to_all x2, blocking collectives, exchange_in_order(): result = lax.all_to_all(result, axes[k], k, k, tiled=True)  7.68 us
    sqrt x17, local copies, waits for them, and re-layouts, phase_angle(): radius = jnp.sqrt(jnp.sum(points * points, axis=-1))  7.16 us
  transfers between devices with their start and end apart: 4, of which 2 were waited for; matrix products, arithmetic and copies ran while one was open for 38% of the time, Pallas kernels for 0%

commit v1 on v0

--- a/solution.py
+++ b/solution.py
@@ -213,8 +213,14 @@
             )
         else:
             moved_array = unfold_pairs(
-                lax.all_to_all(
-                    flatten_pairs(array_now), "sx", split_axis=1, concat_axis=0, tiled=True
+                jnp.concatenate(
+                    lax.all_to_all(
+                        jnp.stack(jnp.split(flatten_pairs(array_now), lax.axis_size("sx"), axis=1)),
+                        "sx",
+                        0,
+                        0,
+                    ),
+                    axis=0,
                 )
             )
             state_in = forward_moved(state_in, moved_array, index_x)

time: 164 us -> 157 us (0.957)
  other arithmetic: 62.9 us -> 59 us
  local copies, waits for them, and re-layouts: 29.5 us -> 26.7 us
    sqrt x17, local copies, waits for them, and re-layouts: 7.16 us -> 4.92 us  [phase_angle(): radius = jnp.sqrt(jnp.sum(points * points, axis=-1))]
    reduce_sum x16, other arithmetic: 4.03 us -> 1.96 us  [phase_angle(): travel = medium[0] + jnp.sum(medium[1:] * centres, axis=-1)]
    all_to_all x1 -> x0, other arithmetic: 1.87 us -> none  [forward_steps(): lax.all_to_all(flatten_pairs(array_now), 'sx', split_axis=1, concat_axis=...]
  transfers between devices with their start and end apart: 4 -> 4, of which waited for: 2 -> 2; matrix products, arithmetic and copies ran while one was open for 38% -> 37% of each run, Pallas kernels for 0% -> 0%
where the time goes in v1:
time: 157 us; the launch traced here: 156 us
  other arithmetic  59 us (38%)
  starting transfers between devices  35.7 us (23%)
  local copies, waits for them, and re-layouts  26.7 us (17%)
  matrix products  16.7 us (11%)
  blocking collectives  7.68 us (5%)
  waiting for transfers between devices  7.42 us (5%)
  between operations  3.18 us (2%)
    all_to_all x2, starting transfers between devices, exchange_in_order(): result = lax.all_to_all(result, axes[k], k, k, tiled=True)  23.1 us
    another operation x38, other arithmetic, box_digits(): return jnp.stack([coord_x, coord_y, coord_z], axis=-1).astype(jnp.float32)  14.1 us
    sub x11, other arithmetic, complex_turn(): real_part * cosine - imag_part * sine_part  13.9 us
    dot_general x4, matrix products, adjoint_level(): jnp.einsum('pkbxhs,cqs->pkbcxhq', stacked, interp, precision=lax.Precisio...  11.2 us
    reduce_sum x4, other arithmetic, adjoint_level(): jnp.sum(back_re, axis=1)  10.8 us
    all_to_all x1, starting transfers between devices, forward_steps(): lax.all_to_all(jnp.stack(jnp.split(flatten_pairs(array_now), lax.axis_siz...  8.18 us
    all_to_all x2, blocking collectives, exchange_in_order(): result = lax.all_to_all(result, axes[k], k, k, tiled=True)  7.68 us
    reduce_sum x14, other arithmetic, phase_angle(): along = jnp.sum(centres * points, axis=-1)  6.48 us
  transfers between devices with their start and end apart: 4, of which 2 were waited for; matrix products, arithmetic and copies ran while one was open for 37% of the time, Pallas kernels for 0%

profile of v1, /device:TPU:2, one launch (start us, length us, event | category | flops | bytes accessed | tf_op | source)
XLA Modules:
  0.0 156.3 jit_solution(17372240812336832314)
XLA Ops:
  1.4 0.6 fusion.288
  2.7 0.7 tile.98
  3.6 0.7 broadcast_in_dim.65
  4.6 0.7 broadcast_in_dim.64
  5.8 0.6 fusion.287
  7.6 0.7 broadcast_multiply_fusion.1
  8.6 1.1 reshape_reshape_broadcast_in_dim.3
  10.9 0.7 multiply_reduce_fusion.8
  12.0 2.1 %convolution_bitcast_fusion.3 = f32[8,8,1,8,2,1,216]{6,1,4,0,3,5,2:T(8,128)S(1)} fusion(f32[8,216,216,1,1]{2,1,4,3,0:T(8,128)S(1)} %copy-done.1, f32[8,8,1,1,1,216]{5,1,3,0,4,2:T(8,128)S(1)} %get-tuple-element.31, f32[8,8,1,1,1,216]{5,1,3,0,4,2:T(8,128)S(1)} %get-tuple-element.30), kind=kOutput, calls=%fused_computation.11 | convolution fusion | flops 573336576 | bytes 2488320 | tf_op jit(solution)/shard_map/pkbxhs,cqs->pkbcxhq/dot_general | solution.py:168
  14.1 2.7 %subtract_reduce_fusion.3 = (f32[8,8,216]{2,0,1:T(8,128)S(1)}, f32[8,8,216]{2,0,1:T(8,128)S(1)}) fusion(f32[8,8,1,8,2,1,216]{6,1,4,0,3,5,2:T(8,128)S(1)} %convolution_bitcast_fusion.3, f32[8,8,8,216]{3,2,1,0:T(8,128)S(1)} %multiply_reduce_fusion.3, f32[8,216]{1,0:T(8,128)S(1)} %sqrt.137, f32[8,8]{1,0:T(8,128)S(1)} %broadcast_add_fusion.6), kind=kLoop, calls=%fused_computation.62 | loop fusion | flops 1299456 | bytes 1444864 | tf_op jit(solution)/shard_map/reduce_sum | solution.py:172
  18.2 2.1 %convolution_bitcast_fusion.2 = f32[1,8,8,8,2,1,216]{6,2,4,1,3,5,0:T(8,128)S(1)} fusion(f32[8,216,216,1,1]{2,1,4,3,0:T(8,128)S(1)} %copy-done.1, f32[1,8,8,1,1,216]{5,2,3,1,4,0:T(8,128)S(1)} %get-tuple-element.27, f32[1,8,8,1,1,216]{5,2,3,1,4,0:T(8,128)S(1)} %get-tuple-element.26), kind=kOutput, calls=%fused_computation.10 | convolution fusion | flops 573336576 | bytes 2488320 | tf_op jit(solution)/shard_map/pkbxhs,cqs->pkbcxhq/dot_general | solution.py:168
  20.3 2.5 %subtract_reduce_fusion.2 = (f32[8,8,216]{2,0,1:T(8,128)S(1)}, f32[8,8,216]{2,0,1:T(8,128)S(1)}) fusion(f32[1,8,8,8,2,1,216]{6,2,4,1,3,5,0:T(8,128)S(1)} %convolution_bitcast_fusion.2, f32[8,8,8,216]{3,2,1,0:T(8,128)S(1)} %multiply_reduce_fusion.2, f32[8,8,216]{2,0,1:T(8,128)S(1)} %copy.436, f32[8]{0:T(128)S(1)} %get-tuple-element.119), kind=kLoop, calls=%fused_computation.59 | loop fusion | flops 1299456 | bytes 1493024 | tf_op jit(solution)/shard_map/reduce_sum | solution.py:172
  23.2 3.8 %all_to_all.40 = f32[16,2,1,2,432]{4,3,0,2,1:T(2,128)S(1)} all-to-all(f32[16,2,1,2,432]{4,3,0,2,1:T(2,128)S(1)} %copy.440), channel_id=1, replica_groups=mesh['sx'=16,'sy_0'=4,'sy_1'=4,'sy_2'=2] {'sy_2'}, dimensions={1} | all-to-all | bytes 221184 | tf_op jit(solution)/shard_map/all_to_all | solution.py:36
  27.1 0.7 copy.441
  27.8 13.3 %all-to-all-start.4 = ((f32[16,2,1,2,432]{4,3,1,2,0:T(2,128)}), f32[16,2,1,2,432]{4,3,1,2,0:T(2,128)S(1)}, u32[]{:S(2)}, u32[]{:S(2)}) async-start(f32[16,2,1,2,432]{4,3,1,2,0:T(2,128)} %copy.441), calls=%async_computation.4 | async-start | bytes 262144 | tf_op jit(solution)/shard_map/all_to_all | solution.py:36
  43.5 0.6 fusion.299
  49.4 0.7 copy.447
  50.4 0.7 multiply_reduce_fusion.23
  51.4 0.7 broadcast_add_fusion
  52.6 0.7 multiply_reduce_fusion.15
  54.6 0.7 multiply_reduce_fusion.24
  57.1 0.6 fusion.443
  61.0 0.7 multiply_reduce_fusion.13
  62.0 2.0 %multiply_subtract_fusion.3 = (f32[1,8,8,8,1,1,216]{6,3,1,4,2,5,0:T(8,128)S(1)}, f32[1,8,8,8,1,1,216]{6,3,1,4,2,5,0:T(8,128)S(1)}) fusion(f32[8,8,8,216]{3,2,1,0:T(8,128)S(1)} %multiply_reduce_fusion.7, f32[8,8,216]{2,0,1:T(8,128)S(1)} %get-tuple-element.111, f32[8,216]{1,0:T(8,128)S(1)} %sqrt.128, f32[8,8]{1,0:T(8,128)S(1)} %broadcast_add_fusion.11, ...), kind=kLoop, calls=%fused_computation.71 | loop fusion | flops 995328 | bytes 1444864 | tf_op jit(solution)/shard_map/sub | solution.py:117
  64.0 1.4 convolution_bitcast_fusion.7
  67.9 1.0 multiply_reduce_fusion.6
  68.9 0.7 multiply_reduce_fusion.16
  70.3 0.6 broadcast_add_fusion.14
  71.6 0.6 sqrt.132
  75.2 0.6 broadcast_add_fusion.4
  76.0 0.6 broadcast_add_fusion.12
  76.7 0.7 multiply_reduce_fusion.9
  77.4 1.0 multiply_reduce_fusion.1
  78.4 0.8 fusion.270
  79.7 8.2 %all-to-all-start = ((f32[16,1,4,432]{3,2,1,0:T(4,128)}), f32[16,1,4,432]{3,2,1,0:T(4,128)}, u32[]{:S(2)}, u32[]{:S(2)}) async-start(f32[16,1,4,432]{3,2,1,0:T(4,128)} %copy-done.9), calls=%async_computation | async-start | bytes 262144 | tf_op jit(solution)/shard_map/all_to_all | solution.py:217
  87.9 0.9 reshape_reshape_reshape_reshape.7
  88.7 1.7 %fusion.428 = (f32[4,8,2,1,1,216]{5,3,2,1,0,4:T(1,128)}, f32[4,8,2,1,1,216]{5,3,2,1,0,4:T(1,128)}) fusion(f32[4,8,2,2,1,216]{5,3,2,1,0,4:T(2,128)} %reshape_reshape_reshape_reshape.7), kind=kLoop, calls=%fused_computation.1382 | loop fusion | bytes 221184 | tf_op jit(solution)/shard_map/slice | solution.py:166
  90.5 6.0 %all-to-all-done = f32[16,1,4,432]{3,2,1,0:T(4,128)} async-done(((f32[16,1,4,432]{3,2,1,0:T(4,128)}), f32[16,1,4,432]{3,2,1,0:T(4,128)}, u32[]{:S(2)}, u32[]{:S(2)}) %all-to-all-start) | async-done | bytes 110624 | tf_op jit(solution)/shard_map/all_to_all | solution.py:217
  96.5 1.1 reshape.11729
  97.7 3.7 %multiply_subtract_fusion.2 = (f32[2,8,4,8,1,1,216]{6,3,1,4,2,0,5:T(8,128)S(1)}, f32[2,8,4,8,1,1,216]{6,3,1,4,2,0,5:T(8,128)S(1)}) fusion(f32[2,8,4,8,216]{4,3,2,1,0:T(8,128)} %multiply_reduce_fusion.6, f32[2,8,4,216]{3,1,2,0:T(8,128)S(1)} %bitcast.642, f32[2,8,216]{2,1,0:T(8,128)} %sqrt.130, f32[4,8]{1,0:T(4,128)} %broadcast_add_fusion.15, ...), kind=kLoop, calls=%fused_computation.69 | loop fusion | flops 995328 | bytes 1451648 | tf_op jit(solution)/shard_map/sub | solution.py:117
  101.5 1.4 convolution_bitcast_fusion.6
  103.4 0.8 mul.4489
  104.2 1.0 reshape.11712
  105.3 3.8 %all_to_all.41 = f32[16,2,2,1,432]{4,2,0,3,1:T(2,128)S(1)} all-to-all(f32[16,2,2,1,432]{4,2,0,3,1:T(2,128)S(1)} %copy.405), channel_id=1, replica_groups=mesh['sx'=16,'sy_0'=4,'sy_1'=4,'sy_2'=2] {'sy_2'}, dimensions={1} | all-to-all | bytes 221184 | tf_op jit(solution)/shard_map/all_to_all | solution.py:36
  109.1 0.7 copy.406
  109.8 9.8 %all-to-all-start.2 = ((f32[16,2,2,1,432]{4,2,1,3,0:T(2,128)}), f32[16,2,2,1,432]{4,2,1,3,0:T(2,128)S(1)}, u32[]{:S(2)}, u32[]{:S(2)}) async-start(f32[16,2,2,1,432]{4,2,1,3,0:T(2,128)} %copy.406), calls=%async_computation.2 | async-start | bytes 262144 | tf_op jit(solution)/shard_map/all_to_all | solution.py:36
  119.6 1.3 multiply_subtract_fusion.5
  120.9 3.5 %convolution_bitcast_fusion.1 = f32[4,8,2,8,2,1,216]{6,1,4,2,0,3,5:T(8,128)S(1)} fusion(f32[8,216,216,1,1,1]{2,1,5,4,3,0:T(8,128)} %constant.2449, f32[4,8,2,1,1,216]{5,1,3,2,0,4:T(8,128)S(1)} %get-tuple-element.37, f32[4,8,2,1,1,216]{5,1,3,2,0,4:T(8,128)S(1)} %get-tuple-element.36), kind=kOutput, calls=%fused_computation.9 | convolution fusion | flops 573336576 | bytes 2488320 | tf_op jit(solution)/shard_map/pkbxhs,cqs->pkbcxhq/dot_general | solution.py:168
  124.4 2.8 %subtract_reduce_fusion.1 = (f32[4,2,8,216]{3,1,0,2:T(2,128)S(1)}, f32[4,2,8,216]{3,1,0,2:T(2,128)S(1)}) fusion(f32[4,8,2,8,2,1,216]{6,1,4,2,0,3,5:T(8,128)S(1)} %convolution_bitcast_fusion.1, f32[4,8,2,8,216]{4,3,2,1,0:T(8,128)S(1)} %copy-done.2, f32[2,8,216]{2,0,1:T(2,128)S(1)} %copy-done.12, f32[4,8]{1,0:T(4,128)S(1)} %copy-done.44), kind=kLoop, calls=%fused_computation.56 | loop fusion | flops 1299456 | bytes 1451648 | tf_op jit(solution)/shard_map/reduce_sum | solution.py:172
  127.4 0.7 copy.477
  128.1 1.7 %reshape.11730 = f32[4,16,432]{2,0,1:T(4,128)} reshape(f32[4,2,8,2,1,216]{5,3,0,2,1,4:T(2,128)} %copy.477) | data formatting | bytes 221184 | tf_op jit(solution)/shard_map/mul | solution.py:172
  129.8 4.4 %all-to-all-start.5 = ((f32[4,16,432]{2,0,1:T(4,128)}), f32[4,16,432]{2,0,1:T(4,128)}, u32[]{:S(2)}, u32[]{:S(2)}) async-start(f32[4,16,432]{2,0,1:T(4,128)} %reshape.11730), calls=%async_computation.5 | async-start | bytes 262144 | tf_op jit(solution)/shard_map/all_to_all | solution.py:242
  134.3 0.9 reshape_reshape_reshape_reshape.6
  135.1 1.1 fusion.430
  136.3 2.9 %multiply_subtract_fusion.1 = (f32[8,8,1,8,1,1,216]{6,3,1,4,0,5,2:T(8,128)S(1)}, f32[8,8,1,8,1,1,216]{6,3,1,4,0,5,2:T(8,128)S(1)}) fusion(f32[8,8,8,216]{3,2,1,0:T(8,128)S(1)} %multiply_reduce_fusion.5, f32[8,8,216]{2,1,0:T(8,128)S(1)} %bitcast.643, f32[8,8,216]{2,1,0:T(8,128)} %sqrt.132, f32[8]{0:T(128)S(1)} %copy-done.61, f32[8,8,216]{2,1,0:T(8,128)S(1)} %bitcast.645), kind=kLoop, calls=%fused_computation.67 | loop fusion | flops 995328 | bytes 1493024 | tf_op jit(solution)/shard_map/sub | solution.py:117
  139.2 1.4 convolution_bitcast_fusion.5
  141.3 1.4 all-to-all-done.5
  142.7 1.1 reshape_reshape.5
  144.2 3.5 %convolution_bitcast_fusion = f32[8,8,1,8,2,1,216]{6,1,0,3,5,4,2:T(8,128)S(1)} fusion(f32[8,216,216,1,1]{2,1,3,0,4:T(8,128)} %constant.2448, f32[8,8,1,1,1,216]{5,1,3,0,4,2:T(8,128)S(1)} %get-tuple-element.29, f32[8,8,1,1,1,216]{5,1,3,0,4,2:T(8,128)S(1)} %get-tuple-element.28), kind=kOutput, calls=%fused_computation.8 | convolution fusion | flops 573336576 | bytes 2488320 | tf_op jit(solution)/shard_map/pkbxhs,cqs->pkbcxhq/dot_general | solution.py:168
  147.8 2.7 %subtract_reduce_fusion = (f32[8,8,216]{2,0,1:T(8,128)S(1)}, f32[8,8,216]{2,0,1:T(8,128)S(1)}) fusion(f32[8,8,1,8,2,1,216]{6,1,0,3,5,4,2:T(8,128)S(1)} %convolution_bitcast_fusion, f32[8,8,8,216]{3,2,1,0:T(8,128)S(1)} %multiply_reduce_fusion, f32[8,216]{1,0:T(8,128)S(1)} %copy-done.14, f32[8,8]{1,0:T(8,128)S(1)} %copy-done.20), kind=kLoop, calls=%fused_computation.53 | loop fusion | flops 1299456 | bytes 1444864 | tf_op jit(solution)/shard_map/reduce_sum | solution.py:172
  150.7 0.8 mul.4773
  151.6 2.0 %multiply_subtract_fusion = (f32[1,8,8,8,1,1,216]{6,3,1,4,2,5,0:T(8,128)S(1)}, f32[1,8,8,8,1,1,216]{6,3,1,4,2,5,0:T(8,128)S(1)}) fusion(f32[8,8,8,216]{3,2,1,0:T(8,128)S(1)} %multiply_reduce_fusion.4, f32[8,8,216]{2,0,1:T(8,128)S(1)} %copy.419, f32[8,216]{1,0:T(8,128)S(1)} %copy-done.15, f32[8,8]{1,0:T(8,128)S(1)} %copy-done.19, f32[8,8,216]{2,0,1:T(8,128)S(1)} %copy.415), kind=kLoop, calls=%fused_computation.65 | loop fusion | flops 995328 | bytes 1444864 | tf_op jit(solution)/shard_map/sub | solution.py:117
  153.7 1.4 convolution_bitcast_fusion.4
  155.5 0.8 mul.4599
  (358 shorter events, 31.0 us)
Async XLA Ops:
  0.6 11.4 %copy-start.1 = (f32[8,216,216,1,1]{2,1,4,3,0:T(8,128)S(1)}, f32[8,216,216,1,1]{2,1,4,3,0:T(8,128)}, u32[]{:S(2)}) copy-start(f32[8,216,216,1,1]{2,1,4,3,0:T(8,128)} %constant.2450) | copy-start | bytes 4478980
  0.6 9.8 %copy-start.11 = (f32[4]{0:T(128)S(1)}, f32[4]{0:T(128)}, u32[]{:S(2)}) copy-start(f32[4]{0:T(128)} %param.22) | copy-start | bytes 52
  8.3 5.8 %copy-start.40 = (f32[3]{0:T(128)}, f32[3]{0:T(128)S(1)}, u32[]{:S(2)}) copy-start(f32[3]{0:T(128)S(1)} %get-tuple-element.67) | copy-start | bytes 40
  8.3 53.5 %copy-start.38 = (f32[3]{0:T(128)}, f32[3]{0:T(128)S(1)}, u32[]{:S(2)}) copy-start(f32[3]{0:T(128)S(1)} %get-tuple-element.70) | copy-start | bytes 40
  8.3 61.9 %copy-start.36 = (f32[3]{0:T(128)}, f32[3]{0:T(128)S(1)}, u32[]{:S(2)}) copy-start(f32[3]{0:T(128)S(1)} %get-tuple-element.68) | copy-start | bytes 40
  8.3 63.9 %copy-start.35 = (f32[3]{0:T(128)}, f32[3]{0:T(128)S(1)}, u32[]{:S(2)}) copy-start(f32[3]{0:T(128)S(1)} %get-tuple-element.69) | copy-start | bytes 40
  8.6 5.5 %copy-start.42 = (f32[216]{0:T(256)}, f32[216]{0:T(256)S(1)}, u32[]{:S(2)}) copy-start(f32[216]{0:T(256)S(1)} %sqrt.135) | copy-start | bytes 2596
  22.8 37.7 %copy-start.10 = (f32[8,8,432]{2,1,0:T(8,128)S(1)}, f32[8,8,432]{2,1,0:T(8,128)}, u32[]{:S(2)}) copy-start(f32[8,8,432]{2,1,0:T(8,128)} %param.20) | copy-start | bytes 331780
  27.8 51.9 %all-to-all-start.4 = ((f32[16,2,1,2,432]{4,3,1,2,0:T(2,128)}), f32[16,2,1,2,432]{4,3,1,2,0:T(2,128)S(1)}, u32[]{:S(2)}, u32[]{:S(2)}) async-start(f32[16,2,1,2,432]{4,3,1,2,0:T(2,128)} %copy.441), calls=%async_computation.4 | async-start | bytes 262144 | tf_op jit(solution)/shard_map/all_to_all | solution.py:36
  59.8 4.2 %copy-start = (f32[8,216,216,1,1]{2,1,0,4,3:T(8,128)S(1)}, f32[8,216,216,1,1]{2,1,0,4,3:T(8,128)}, u32[]{:S(2)}) copy-start(f32[8,216,216,1,1]{2,1,0,4,3:T(8,128)} %constant.2446) | copy-start | bytes 4478980
  66.0 5.7 %copy-start.4 = (f32[8,8,216]{2,1,0:T(8,128)S(1)}, f32[8,8,216]{2,1,0:T(8,128)}, u32[]{:S(2)}) copy-start(f32[8,8,216]{2,1,0:T(8,128)} %multiply_reduce_fusion.15) | copy-start | bytes 165892
  66.0 6.3 %copy-start.59 = (s32[1,1,1,8,1,1]{3,5,4,2,1,0:T(1,128)S(1)}, s32[1,1,1,8,1,1]{3,5,4,2,1,0:T(1,128)}, u32[]{:S(2)}) copy-start(s32[1,1,1,8,1,1]{3,5,4,2,1,0:T(1,128)} %get-tuple-element.110) | copy-start | bytes 100
  66.0 6.3 %copy-start.60 = (s32[1,1,1,8,1,1]{3,5,4,2,1,0:T(1,128)S(1)}, s32[1,1,1,8,1,1]{3,5,4,2,1,0:T(1,128)}, u32[]{:S(2)}) copy-start(s32[1,1,1,8,1,1]{3,5,4,2,1,0:T(1,128)} %fusion.426) | copy-start | bytes 100
  66.0 7.0 %copy-start.18 = (f32[8,216]{1,0:T(8,128)S(1)}, f32[8,216]{1,0:T(8,128)}, u32[]{:S(2)}) copy-start(f32[8,216]{1,0:T(8,128)} %multiply_reduce_fusion.24) | copy-start | bytes 20740
  66.0 7.0 %copy-start.17 = (f32[8,216]{1,0:T(8,128)S(1)}, f32[8,216]{1,0:T(8,128)}, u32[]{:S(2)}) copy-start(f32[8,216]{1,0:T(8,128)} %get-tuple-element.12) | copy-start | bytes 20740
  66.0 7.6 %copy-start.23 = (s32[1,1,8,8,1,1]{3,2,5,4,1,0:T(8,128)S(1)}, s32[1,1,8,8,1,1]{3,2,5,4,1,0:T(8,128)}, u32[]{:S(2)}) copy-start(s32[1,1,8,8,1,1]{3,2,5,4,1,0:T(8,128)} %get-tuple-element.102) | copy-start | bytes 772
  66.0 7.6 %copy-start.24 = (s32[1,1,8,8,1,1]{3,2,5,4,1,0:T(8,128)S(1)}, s32[1,1,8,8,1,1]{3,2,5,4,1,0:T(8,128)}, u32[]{:S(2)}) copy-start(s32[1,1,8,8,1,1]{3,2,5,4,1,0:T(8,128)} %get-tuple-element.98) | copy-start | bytes 772
  66.0 7.6 %copy-start.32 = (s32[1,1,8,8,1,1]{3,2,5,4,1,0:T(8,128)S(1)}, s32[1,1,8,8,1,1]{3,2,5,4,1,0:T(8,128)}, u32[]{:S(2)}) copy-start(s32[1,1,8,8,1,1]{3,2,5,4,1,0:T(8,128)} %fusion.444) | copy-start | bytes 772
  66.0 7.6 %copy-start.41 = (f32[3]{0:T(128)S(1)}, f32[3]{0:T(128)}, u32[]{:S(2)}) copy-start(f32[3]{0:T(128)} %copy-done.40) | copy-start | bytes 40
  66.0 8.3 %copy-start.21 = (s32[1,8,8,1,1]{2,1,4,3,0:T(8,128)S(1)}, s32[1,8,8,1,1]{2,1,4,3,0:T(8,128)}, u32[]{:S(2)}) copy-start(s32[1,8,8,1,1]{2,1,4,3,0:T(8,128)} %get-tuple-element.104) | copy-start | bytes 772
  66.1 8.3 %copy-start.22 = (s32[1,8,8,1,1]{2,1,4,3,0:T(8,128)S(1)}, s32[1,8,8,1,1]{2,1,4,3,0:T(8,128)}, u32[]{:S(2)}) copy-start(s32[1,8,8,1,1]{2,1,4,3,0:T(8,128)} %get-tuple-element.100) | copy-start | bytes 772
  66.1 8.2 %copy-start.31 = (s32[1,8,8,1,1]{2,1,4,3,0:T(8,128)S(1)}, s32[1,8,8,1,1]{2,1,4,3,0:T(8,128)}, u32[]{:S(2)}) copy-start(s32[1,8,8,1,1]{2,1,4,3,0:T(8,128)} %fusion.443) | copy-start | bytes 772
  66.1 8.9 %copy-start.28 = (s32[8,8,1,1,1]{1,0,4,3,2:T(8,128)S(1)}, s32[8,8,1,1,1]{1,0,4,3,2:T(8,128)}, u32[]{:S(2)}) copy-start(s32[8,8,1,1,1]{1,0,4,3,2:T(8,128)} %fusion.298) | copy-start | bytes 772
  66.1 8.9 %copy-start.29 = (s32[8,8,1,1,1]{1,0,4,3,2:T(8,128)S(1)}, s32[8,8,1,1,1]{1,0,4,3,2:T(8,128)}, u32[]{:S(2)}) copy-start(s32[8,8,1,1,1]{1,0,4,3,2:T(8,128)} %fusion.300) | copy-start | bytes 772
  66.1 8.9 %copy-start.30 = (s32[8,8,1,1,1]{1,0,4,3,2:T(8,128)S(1)}, s32[8,8,1,1,1]{1,0,4,3,2:T(8,128)}, u32[]{:S(2)}) copy-start(s32[8,8,1,1,1]{1,0,4,3,2:T(8,128)} %fusion.302) | copy-start | bytes 772
  66.1 8.9 %copy-start.39 = (f32[3]{0:T(128)S(1)}, f32[3]{0:T(128)}, u32[]{:S(2)}) copy-start(f32[3]{0:T(128)} %copy-done.38) | copy-start | bytes 40
  66.1 9.0 %copy-start.25 = (s32[8,8,1,1,1,1]{1,0,5,4,3,2:T(8,128)S(1)}, s32[8,8,1,1,1,1]{1,0,5,4,3,2:T(8,128)}, u32[]{:S(2)}) copy-start(s32[8,8,1,1,1,1]{1,0,5,4,3,2:T(8,128)} %fusion.297) | copy-start | bytes 772
  66.1 9.0 %copy-start.26 = (s32[8,8,1,1,1,1]{1,0,5,4,3,2:T(8,128)S(1)}, s32[8,8,1,1,1,1]{1,0,5,4,3,2:T(8,128)}, u32[]{:S(2)}) copy-start(s32[8,8,1,1,1,1]{1,0,5,4,3,2:T(8,128)} %fusion.299) | copy-start | bytes 772
  66.1 9.0 %copy-start.27 = (s32[8,8,1,1,1,1]{1,0,5,4,3,2:T(8,128)S(1)}, s32[8,8,1,1,1,1]{1,0,5,4,3,2:T(8,128)}, u32[]{:S(2)}) copy-start(s32[8,8,1,1,1,1]{1,0,5,4,3,2:T(8,128)} %fusion.301) | copy-start | bytes 772
  66.1 9.7 %copy-start.48 = (s32[4,8,1,1,1,1]{1,0,5,4,3,2:T(4,128)S(1)}, s32[4,8,1,1,1,1]{1,0,5,4,3,2:T(4,128)}, u32[]{:S(2)}) copy-start(s32[4,8,1,1,1,1]{1,0,5,4,3,2:T(4,128)} %fusion.329) | copy-start | bytes 388
  66.2 9.7 %copy-start.49 = (s32[4,8,1,1,1,1]{1,0,5,4,3,2:T(4,128)S(1)}, s32[4,8,1,1,1,1]{1,0,5,4,3,2:T(4,128)}, u32[]{:S(2)}) copy-start(s32[4,8,1,1,1,1]{1,0,5,4,3,2:T(4,128)} %fusion.331) | copy-start | bytes 388
  66.2 9.7 %copy-start.50 = (s32[4,8,1,1,1,1]{1,0,5,4,3,2:T(4,128)S(1)}, s32[4,8,1,1,1,1]{1,0,5,4,3,2:T(4,128)}, u32[]{:S(2)}) copy-start(s32[4,8,1,1,1,1]{1,0,5,4,3,2:T(4,128)} %fusion.333) | copy-start | bytes 388
  66.2 9.8 %copy-start.45 = (s32[4,8,1,1,1]{1,0,4,3,2:T(4,128)S(1)}, s32[4,8,1,1,1]{1,0,4,3,2:T(4,128)}, u32[]{:S(2)}) copy-start(s32[4,8,1,1,1]{1,0,4,3,2:T(4,128)} %fusion.330) | copy-start | bytes 388
  66.2 9.7 %copy-start.46 = (s32[4,8,1,1,1]{1,0,4,3,2:T(4,128)S(1)}, s32[4,8,1,1,1]{1,0,4,3,2:T(4,128)}, u32[]{:S(2)}) copy-start(s32[4,8,1,1,1]{1,0,4,3,2:T(4,128)} %fusion.332) | copy-start | bytes 388
  66.2 9.7 %copy-start.47 = (s32[4,8,1,1,1]{1,0,4,3,2:T(4,128)S(1)}, s32[4,8,1,1,1]{1,0,4,3,2:T(4,128)}, u32[]{:S(2)}) copy-start(s32[4,8,1,1,1]{1,0,4,3,2:T(4,128)} %fusion.334) | copy-start | bytes 388
  66.2 10.5 %copy-start.16 = (f32[4,8,3]{1,2,0:T(4,128)S(1)}, f32[4,8,3]{1,2,0:T(4,128)}, u32[]{:S(2)}) copy-start(f32[4,8,3]{1,2,0:T(4,128)} %copy.443) | copy-start | bytes 1156
  66.2 11.1 %copy-start.8 = (f32[2,8,216,3]{2,1,3,0:T(8,128)S(1)}, f32[2,8,216,3]{2,1,3,0:T(8,128)}, u32[]{:S(2)}) copy-start(f32[2,8,216,3]{2,1,3,0:T(8,128)} %get-tuple-element.54) | copy-start | bytes 124420
  66.3 11.1 %copy-start.13 = (f32[4,8,3]{2,1,0:T(8,128)S(1)}, f32[4,8,3]{2,1,0:T(8,128)}, u32[]{:S(2)}) copy-start(f32[4,8,3]{2,1,0:T(8,128)} %copy.447) | copy-start | bytes 1156
  66.5 4.6 %copy-start.9 = (f32[16,1,4,432]{3,2,1,0:T(4,128)}, f32[16,1,4,432]{3,2,1,0:T(4,128)S(1)}, u32[]{:S(2)}) copy-start(f32[16,1,4,432]{3,2,1,0:T(4,128)S(1)} %constant_dynamic-update-slice_fusion) | copy-start | bytes 331780
  67.9 10.5 %copy-start.56 = (s32[1,1,8,1,1]{2,4,3,1,0:T(1,128)S(1)}, s32[1,1,8,1,1]{2,4,3,1,0:T(1,128)}, u32[]{:S(2)}) copy-start(s32[1,1,8,1,1]{2,4,3,1,0:T(1,128)} %get-tuple-element.107) | copy-start | bytes 100
  67.9 10.5 %copy-start.57 = (s32[1,1,8,1,1]{2,4,3,1,0:T(1,128)S(1)}, s32[1,1,8,1,1]{2,4,3,1,0:T(1,128)}, u32[]{:S(2)}) copy-start(s32[1,1,8,1,1]{2,4,3,1,0:T(1,128)} %get-tuple-element.108) | copy-start | bytes 100
  67.9 10.5 %copy-start.58 = (s32[1,1,8,1,1]{2,4,3,1,0:T(1,128)S(1)}, s32[1,1,8,1,1]{2,4,3,1,0:T(1,128)}, u32[]{:S(2)}) copy-start(s32[1,1,8,1,1]{2,4,3,1,0:T(1,128)} %fusion.425) | copy-start | bytes 100
  70.3 5.5 %copy-start.37 = (f32[3]{0:T(128)S(1)}, f32[3]{0:T(128)}, u32[]{:S(2)}) copy-start(f32[3]{0:T(128)} %copy-done.36) | copy-start | bytes 40
  79.7 16.8 %all-to-all-start = ((f32[16,1,4,432]{3,2,1,0:T(4,128)}), f32[16,1,4,432]{3,2,1,0:T(4,128)}, u32[]{:S(2)}, u32[]{:S(2)}) async-start(f32[16,1,4,432]{3,2,1,0:T(4,128)} %copy-done.9), calls=%async_computation | async-start | bytes 262144 | tf_op jit(solution)/shard_map/all_to_all | solution.py:217
  97.6 3.9 %copy-start.3 = (f32[8,216,216,1,1,1]{2,1,0,5,4,3:T(8,128)S(1)}, f32[8,216,216,1,1,1]{2,1,0,5,4,3:T(8,128)}, u32[]{:S(2)}) copy-start(f32[8,216,216,1,1,1]{2,1,0,5,4,3:T(8,128)} %constant.2447) | copy-start | bytes 4478980
  101.5 1.4 copy-start.5
  101.5 1.4 copy-start.52
  101.5 1.4 copy-start.53
  102.9 16.6 %copy-start.51 = (f32[4,8]{1,0:T(4,128)S(1)}, f32[4,8]{1,0:T(4,128)}, u32[]{:S(2)}) copy-start(f32[4,8]{1,0:T(4,128)} %get-tuple-element.118) | copy-start | bytes 388
  109.8 14.6 %copy-start.44 = (f32[4,8]{1,0:T(4,128)S(1)}, f32[4,8]{1,0:T(4,128)}, u32[]{:S(2)}) copy-start(f32[4,8]{1,0:T(4,128)} %get-tuple-element.117) | copy-start | bytes 388
  109.8 20.0 %all-to-all-start.2 = ((f32[16,2,2,1,432]{4,2,1,3,0:T(2,128)}), f32[16,2,2,1,432]{4,2,1,3,0:T(2,128)S(1)}, u32[]{:S(2)}, u32[]{:S(2)}) async-start(f32[16,2,2,1,432]{4,2,1,3,0:T(2,128)} %copy.406), calls=%async_computation.2 | async-start | bytes 262144 | tf_op jit(solution)/shard_map/all_to_all | solution.py:36
  119.5 4.9 %copy-start.2 = (f32[4,8,2,8,216]{4,3,2,1,0:T(8,128)S(1)}, f32[4,8,2,8,216]{4,3,2,1,0:T(8,128)}, u32[]{:S(2)}) copy-start(f32[4,8,2,8,216]{4,3,2,1,0:T(8,128)} %multiply_reduce_fusion.1) | copy-start | bytes 1327108
  119.5 4.9 %copy-start.12 = (f32[2,8,216]{2,0,1:T(2,128)S(1)}, f32[2,8,216]{2,0,1:T(2,128)}, u32[]{:S(2)}) copy-start(f32[2,8,216]{2,0,1:T(2,128)} %copy.451) | copy-start | bytes 41476
  124.4 11.8 %copy-start.61 = (f32[8]{0:T(128)S(1)}, f32[8]{0:T(128)}, u32[]{:S(2)}) copy-start(f32[8]{0:T(128)} %broadcast_add_fusion.19) | copy-start | bytes 100
  129.8 12.8 %all-to-all-start.5 = ((f32[4,16,432]{2,0,1:T(4,128)}), f32[4,16,432]{2,0,1:T(4,128)}, u32[]{:S(2)}, u32[]{:S(2)}) async-start(f32[4,16,432]{2,0,1:T(4,128)} %reshape.11730), calls=%async_computation.5 | async-start | bytes 262144 | tf_op jit(solution)/shard_map/all_to_all | solution.py:242
  139.2 1.4 copy-start.55
  139.2 4.7 %copy-start.6 = (f32[8,8,216]{2,1,0:T(8,128)S(1)}, f32[8,8,216]{2,1,0:T(8,128)}, u32[]{:S(2)}) copy-start(f32[8,8,216]{2,1,0:T(8,128)} %get-tuple-element.77) | copy-start | bytes 165892
  139.2 4.7 %copy-start.34 = (f32[8,8]{1,0:T(8,128)S(1)}, f32[8,8]{1,0:T(8,128)}, u32[]{:S(2)}) copy-start(f32[8,8]{1,0:T(8,128)} %get-tuple-element.116) | copy-start | bytes 772
  139.2 4.7 %copy-start.54 = (f32[216]{0:T(256)S(1)}, f32[216]{0:T(256)}, u32[]{:S(2)}) copy-start(f32[216]{0:T(256)} %sqrt.142) | copy-start | bytes 2596
  143.7 4.1 %copy-start.14 = (f32[8,216]{1,0:T(8,128)S(1)}, f32[8,216]{1,0:T(8,128)}, u32[]{:S(2)}) copy-start(f32[8,216]{1,0:T(8,128)} %sqrt.143) | copy-start | bytes 20740
  143.8 4.1 %copy-start.20 = (f32[8,8]{1,0:T(8,128)S(1)}, f32[8,8]{1,0:T(8,128)}, u32[]{:S(2)}) copy-start(f32[8,8]{1,0:T(8,128)} %get-tuple-element.115) | copy-start | bytes 772
  147.8 3.8 %copy-start.15 = (f32[8,216]{1,0:T(8,128)S(1)}, f32[8,216]{1,0:T(8,128)}, u32[]{:S(2)}) copy-start(f32[8,216]{1,0:T(8,128)} %sqrt.134) | copy-start | bytes 20740
  147.8 3.8 %copy-start.19 = (f32[8,8]{1,0:T(8,128)S(1)}, f32[8,8]{1,0:T(8,128)}, u32[]{:S(2)}) copy-start(f32[8,8]{1,0:T(8,128)} %broadcast_add_fusion.9) | copy-start | bytes 772
  153.6 1.4 copy-start.7
  (2 other events, 2.8 us)
